TPU v7x, 32 devices: a whole 2x2x4 slice. The times are simulated.
32 devices in a mesh: row: 4 (over z), col: 8 (over y, x, core).
Axes of the slice: x: 2, y: 2, z: 4, core: 2. Of those that a mesh axis runs over, the one named last changes fastest.
Arguments:
- tokens: bfloat16 [128, 4096], P(('row', 'col')), may hold values from -24 to 24
- counts: int32 [32], P(('row', 'col')), may hold values from 1 to 4, 104 in all
- cotangent: bfloat16 [128, 4096], P(('row', 'col')), may hold values from -6 to 6
- up_weight: bfloat16 [2, 4096, 16384], P(None, 'col', 'row'), may hold values from -0.09375 to 0.09375
- down_weight: bfloat16 [2, 16384, 4096], P(None, 'row', 'col'), may hold values from -0.046875 to 0.046875
- norm_gain: float32 [2, 4096], P(None, 'col'), may hold values from 0.5 to 2
Outputs:
- token_grad: bfloat16 [128, 4096], P(('row', 'col'))
- up_grad: float32 [2, 4096, 16384], P(None, 'col', 'row')
- down_grad: float32 [2, 16384, 4096], P(None, 'row', 'col')
- gain_grad: float32 [2, 4096], P(None, 'col')
All inputs are finite; a program needn't handle non-finite values. No bound on the sum of `counts` on one device may be relied on, other than what follows from the above.
Results may differ from a plain program's by a relative error of at most 0.0095.
Values may be sent and summed in bfloat16 or wider, within the bound.
A program may use at most 128 MiB of HBM per device.

v0:
```python
import jax
import jax.numpy as jnp
from jax import lax
from jax.sharding import PartitionSpec as P

D = 4096


epsilon_norm = 1e-06
gelu_scale = 0.7978845608028654
cubic_term = 0.044715
contract_rows = (((0,), (0,)), ((), ()))
contract_cols = (((1,), (1,)), ((), ()))


def gelu_value(pre_act):
    tangent = jnp.tanh(gelu_scale * (pre_act + cubic_term * pre_act * pre_act * pre_act))
    return 0.5 * pre_act * (1.0 + tangent)


def gelu_slope(pre_act):
    tangent = jnp.tanh(gelu_scale * (pre_act + cubic_term * pre_act * pre_act * pre_act))
    return 0.5 * (1.0 + tangent) + 0.5 * pre_act * (1.0 - tangent * tangent) * gelu_scale * (
        1.0 + 3.0 * cubic_term * pre_act * pre_act
    )


def on_device(tokens, counts, cotangent, up_weight, down_weight, norm_gain):
    slot_total = tokens.shape[0]
    live_slots = (jnp.arange(slot_total, dtype=jnp.int32) < counts[0]).astype(jnp.bfloat16)[:, None]
    entry_tokens, entry_grads = (
        lax.all_to_all(tokens, "col", split_axis=1, concat_axis=0, tiled=True),
        lax.all_to_all(cotangent * live_slots, "col", split_axis=1, concat_axis=0, tiled=True),
    )
    stream = entry_tokens.astype(jnp.float32)
    layer_total = up_weight.shape[0]
    saved = []
    for layer_index in range(layer_total):
        gain_part = norm_gain[layer_index][None, :]
        up_block = up_weight[layer_index]
        down_block = down_weight[layer_index]
        square_sum = lax.psum(jnp.sum(stream * stream, axis=1), "col")
        scale_rows = lax.rsqrt(square_sum / D + epsilon_norm)[:, None]
        normed = (stream * scale_rows * gain_part).astype(jnp.bfloat16)
        normed_all = lax.all_gather(normed, "row", axis=0, tiled=True)
        pre_rows = lax.psum_scatter(
            jnp.dot(normed_all, up_block, preferred_element_type=jnp.float32),
            "col",
            scatter_dimension=0,
            tiled=True,
        )
        hidden_all = lax.all_gather(
            gelu_value(pre_rows).astype(jnp.bfloat16), "col", axis=0, tiled=True
        )
        slope_rows = gelu_slope(pre_rows)
        saved.append((stream, scale_rows, normed_all, hidden_all, slope_rows))
        stream = stream + lax.psum_scatter(
            jnp.dot(hidden_all, down_block, preferred_element_type=jnp.float32),
            "row",
            scatter_dimension=0,
            tiled=True,
        )
    grad_stream = entry_grads.astype(jnp.float32)
    up_grads = []
    down_grads = []
    gain_grads = []
    for layer_index in reversed(range(layer_total)):
        stream_in, scale_rows, normed_all, hidden_all, slope_rows = saved[layer_index]
        gain_part = norm_gain[layer_index][None, :]
        up_block = up_weight[layer_index]
        down_block = down_weight[layer_index]
        grad_all = lax.all_gather(grad_stream.astype(jnp.bfloat16), "row", axis=0, tiled=True)
        down_grads.append(
            lax.dot_general(hidden_all, grad_all, contract_rows, preferred_element_type=jnp.float32)
        )
        grad_hidden = lax.psum_scatter(
            lax.dot_general(
                grad_all, down_block, contract_cols, preferred_element_type=jnp.float32
            ),
            "col",
            scatter_dimension=0,
            tiled=True,
        )
        grad_pre = (grad_hidden * slope_rows).astype(jnp.bfloat16)
        grad_pre_all = lax.all_gather(grad_pre, "col", axis=0, tiled=True)
        up_grads.append(
            lax.dot_general(
                normed_all, grad_pre_all, contract_rows, preferred_element_type=jnp.float32
            )
        )
        grad_normed = lax.psum_scatter(
            lax.dot_general(
                grad_pre_all, up_block, contract_cols, preferred_element_type=jnp.float32
            ),
            "row",
            scatter_dimension=0,
            tiled=True,
        )
        unit_rows = stream_in * scale_rows
        weighted = grad_normed * gain_part
        inner_sum = lax.psum(jnp.sum(weighted * unit_rows, axis=1), "col")
        gain_grads.append(lax.psum(jnp.sum(grad_normed * unit_rows, axis=0), "row"))
        grad_stream = grad_stream + scale_rows * (weighted - unit_rows * (inner_sum / D)[:, None])
    token_grad = lax.all_to_all(
        grad_stream.astype(jnp.bfloat16), "col", split_axis=0, concat_axis=1, tiled=True
    )
    return (
        token_grad,
        jnp.stack(up_grads[::-1]),
        jnp.stack(down_grads[::-1]),
        jnp.stack(gain_grads[::-1]),
    )


def solution(mesh):
    placed = (
        P(("row", "col"), None),
        P(("row", "col")),
        P(("row", "col"), None),
        P(None, "col", "row"),
        P(None, "row", "col"),
        P(None, "col"),
    )
    return jax.shard_map(
        on_device,
        mesh=mesh,
        in_specs=placed,
        out_specs=(
            P(("row", "col"), None),
            P(None, "col", "row"),
            P(None, "row", "col"),
            P(None, "col"),
        ),
        check_vma=False,
    )
```

profile of v0, /device:TPU:0, one launch (start us, length us, event | category | flops | bytes accessed | tf_op | source)
XLA Modules:
  0.0 463.6 jit_solution(11648052498002188841)
XLA Ops:
  7.2 5.2 %all-to-all-start.1 = ((bf16[4,8,512]{2,0,1:T(4,128)(2,1)}), bf16[4,8,512]{2,0,1:T(4,128)(2,1)S(1)}, u32[]{:S(2)}, u32[]{:S(2)}) async-start(bf16[4,8,512]{2,0,1:T(4,128)(2,1)} %bitcast.66), calls=%async_computation.1 | async-start | bytes 65536 | tf_op jit(solution)/shard_map/all_to_all | solution.py:32
  12.4 0.8 fusion.37
  13.2 4.0 all-to-all-done.1
  17.4 12.0 %psum.42 = f32[32]{0:T(128)S(1)} all-reduce(f32[32]{0:T(128)S(1)} %reduce_sum.60), channel_id=1, replica_groups=mesh['row'=4,'col'=8] {'col'}, use_global_device_ids=true, to_apply=%region_1.0 | all-reduce | flops 32 | bytes 256 | tf_op jit(solution)/shard_map/psum | solution.py:42
  29.5 13.6 %all_gather.24 = bf16[128,512]{1,0:T(8,128)(2,1)S(1)} all-gather(bf16[32,512]{1,0:T(8,128)(2,1)S(1)} %multiply_convert_fusion.3), channel_id=1, replica_groups=mesh['row'=4,'col'=8] {'row'}, dimensions={0}, use_global_device_ids=true | all-gather | bytes 163840 | tf_op jit(solution)/shard_map/all_gather | solution.py:45
  43.1 4.2 fusion.12
  47.4 41.4 %reduce-scatter.8.cloned.1.call-done = f32[16,4096]{1,0:T(8,128)} async-done(((f32[128,4096]{1,0:T(8,128)}), f32[16,4096]{1,0:T(8,128)}) %reduce-scatter.8.cloned.1.call-update) | async-done | bytes 262160 | tf_op jit(solution)/shard_map/reduce_scatter | solution.py:46
  88.7 1.7 multiply_convert_fusion.1
  91.2 23.7 %all-gather.5.cloned.1.call-done = bf16[128,4096]{1,0:T(8,128)(2,1)} async-done(((bf16[16,4096]{1,0:T(8,128)(2,1)}), bf16[128,4096]{1,0:T(8,128)(2,1)}) %all-gather.5.cloned.1.call-update) | async-done | bytes 1048592 | tf_op jit(solution)/shard_map/all_gather | solution.py:52
  114.9 3.9 fusion.8
  119.0 7.4 %all_to_all.51 = bf16[4,8,512]{2,0,1:T(4,128)(2,1)S(1)} all-to-all(bf16[4,8,512]{2,0,1:T(4,128)(2,1)S(1)} %bitcast.57), channel_id=1, replica_groups=mesh['row'=4,'col'=8] {'col'}, dimensions={1} | all-to-all | bytes 65536 | tf_op jit(solution)/shard_map/all_to_all | solution.py:33
  126.4 13.8 %all_gather.26 = bf16[128,512]{1,0:T(8,128)(2,1)S(1)} all-gather(bf16[32,512]{1,0:T(8,128)(2,1)S(1)} %all_to_all.41), channel_id=1, replica_groups=mesh['row'=4,'col'=8] {'row'}, dimensions={0}, use_global_device_ids=true | all-gather | bytes 163840 | tf_op jit(solution)/shard_map/all_gather | solution.py:72
  140.2 5.0 %fusion.4 = f32[128,4096]{1,0:T(8,128)} fusion(bf16[128,512]{1,0:T(8,128)(2,1)S(1)} %all_gather.26, bf16[2,4096,512]{2,1,0:T(8,128)(2,1)} %param.10), kind=kOutput, calls=%fused_computation.10 | convolution fusion | flops 536870912 | bytes 6422528 | tf_op jit(solution)/shard_map/dot_general | solution.py:77
  145.3 1.0 multiply_reduce_fusion.4
  146.2 11.8 %psum.43 = f32[32]{0:T(128)S(1)} all-reduce(f32[32]{0:T(128)S(1)} %get-tuple-element.10), channel_id=1, replica_groups=mesh['row'=4,'col'=8] {'col'}, use_global_device_ids=true, to_apply=%region_5.0 | all-reduce | flops 32 | bytes 256 | tf_op jit(solution)/shard_map/psum | solution.py:42
  158.1 13.5 %all_gather.27 = bf16[128,512]{1,0:T(8,128)(2,1)S(1)} all-gather(bf16[32,512]{1,0:T(8,128)(2,1)S(1)} %multiply_convert_fusion.2), channel_id=1, replica_groups=mesh['row'=4,'col'=8] {'row'}, dimensions={0}, use_global_device_ids=true | all-gather | bytes 163840 | tf_op jit(solution)/shard_map/all_gather | solution.py:45
  171.6 4.3 fusion.2
  175.9 10.3 %reduce-scatter.12.cloned.1.call-done = f32[16,4096]{1,0:T(8,128)} async-done(((f32[128,4096]{1,0:T(8,128)}), f32[16,4096]{1,0:T(8,128)}) %reduce-scatter.12.cloned.1.call-update) | async-done | bytes 262160 | tf_op jit(solution)/shard_map/reduce_scatter | solution.py:76
  186.2 45.4 %reduce-scatter.14.cloned.1.call-done = f32[16,4096]{1,0:T(8,128)} async-done(((f32[128,4096]{1,0:T(8,128)}), f32[16,4096]{1,0:T(8,128)}) %reduce-scatter.14.cloned.1.call-update) | async-done | bytes 262160 | tf_op jit(solution)/shard_map/reduce_scatter | solution.py:46
  231.6 1.9 multiply_convert_fusion
  233.6 23.8 %all-gather.7.cloned.1.call-done = bf16[128,4096]{1,0:T(8,128)(2,1)} async-done(((bf16[16,4096]{1,0:T(8,128)(2,1)}), bf16[128,4096]{1,0:T(8,128)(2,1)}) %all-gather.7.cloned.1.call-update) | async-done | bytes 1048592 | tf_op jit(solution)/shard_map/all_gather | solution.py:85
  257.4 4.8 %fusion = f32[128,512]{1,0:T(8,128)} fusion(bf16[128,4096]{1,0:T(8,128)(2,1)} %all-gather.7.cloned.1.call-done, bf16[2,512,4096]{2,1,0:T(8,128)(2,1)} %param.9), kind=kOutput, calls=%fused_computation.6 | convolution fusion | flops 536870912 | bytes 5505024 | tf_op jit(solution)/shard_map/dot_general | solution.py:92
  262.3 19.7 %reduce-scatter.16.cloned.1.call-done = f32[32,512]{1,0:T(8,128)} async-done(((f32[128,512]{1,0:T(8,128)}), f32[32,512]{1,0:T(8,128)}) %reduce-scatter.16.cloned.1.call-update) | async-done | bytes 65552 | tf_op jit(solution)/shard_map/reduce_scatter | solution.py:91
  282.1 1.0 multiply_reduce_fusion
  283.1 12.0 %psum.44 = f32[32]{0:T(128)S(1)} all-reduce(f32[32]{0:T(128)S(1)} %get-tuple-element.7), channel_id=1, replica_groups=mesh['row'=4,'col'=8] {'col'}, use_global_device_ids=true, to_apply=%region_10.0 | all-reduce | flops 32 | bytes 256 | tf_op jit(solution)/shard_map/psum | solution.py:101
  295.1 0.9 fusion.36
  296.0 13.6 %all_gather.29 = bf16[128,512]{1,0:T(8,128)(2,1)S(1)} all-gather(bf16[32,512]{1,0:T(8,128)(2,1)S(1)} %fusion.36), channel_id=1, replica_groups=mesh['row'=4,'col'=8] {'row'}, dimensions={0}, use_global_device_ids=true | all-gather | bytes 163840 | tf_op jit(solution)/shard_map/all_gather | solution.py:72
  309.6 5.0 %fusion.6 = f32[128,4096]{1,0:T(8,128)} fusion(bf16[128,512]{1,0:T(8,128)(2,1)S(1)} %all_gather.29, bf16[2,4096,512]{2,1,0:T(8,128)(2,1)} %param.10), kind=kOutput, calls=%fused_computation.12 | convolution fusion | flops 536870912 | bytes 6422528 | tf_op jit(solution)/shard_map/dot_general | solution.py:77
  314.7 0.7 all-gather.11.cloned.1.call-update
  315.4 37.6 %reduce-scatter.18.cloned.1.call-done = f32[16,4096]{1,0:T(8,128)} async-done(((f32[128,4096]{1,0:T(8,128)}), f32[16,4096]{1,0:T(8,128)}) %reduce-scatter.18.cloned.1.call-update) | async-done | bytes 262160 | tf_op jit(solution)/shard_map/reduce_scatter | solution.py:76
  353.0 1.8 fusion.34
  355.1 4.5 convolution_bitcast_fusion.2
  359.6 19.5 %all-gather.11.cloned.1.call-done = bf16[128,4096]{1,0:T(8,128)(2,1)} async-done(((bf16[16,4096]{1,0:T(8,128)(2,1)}), bf16[128,4096]{1,0:T(8,128)(2,1)}) %all-gather.11.cloned.1.call-update) | async-done | bytes 1048592 | tf_op jit(solution)/shard_map/all_gather | solution.py:52
  379.0 2.5 convolution_bitcast_fusion
  381.5 1.3 convolution_bitcast_fusion.1
  382.8 6.4 %pad_maximum_fusion.1 = f32[2,4096,512]{2,1,0:T(8,128)} fusion(f32[1,4096,512]{2,1,0:T(8,128)S(1)} %convolution_bitcast_fusion, f32[1,4096,512]{2,1,0:T(8,128)S(1)} %convolution_bitcast_fusion.1), kind=kLoop, calls=%fused_computation.1 | loop fusion | flops 4194304 | bytes 33554432 | tf_op jit(solution)/shard_map/stack | solution.py:110
  389.2 15.1 %all-gather.9.cloned.1.call-done = bf16[128,4096]{1,0:T(8,128)(2,1)} async-done(((bf16[16,4096]{1,0:T(8,128)(2,1)}), bf16[128,4096]{1,0:T(8,128)(2,1)}) %all-gather.9.cloned.1.call-update) | async-done | bytes 1048592 | tf_op jit(solution)/shard_map/all_gather | solution.py:85
  404.3 4.8 %fusion.10 = f32[128,512]{1,0:T(8,128)} fusion(bf16[128,4096]{1,0:T(8,128)(2,1)} %all-gather.9.cloned.1.call-done, bf16[2,512,4096]{2,1,0:T(8,128)(2,1)} %param.9), kind=kOutput, calls=%fused_computation.16 | convolution fusion | flops 536870912 | bytes 5505024 | tf_op jit(solution)/shard_map/dot_general | solution.py:92
  409.1 2.5 convolution_bitcast_fusion.3
  411.6 9.8 %pad_maximum_fusion = f32[2,512,4096]{2,1,0:T(8,128)} fusion(f32[1,512,4096]{2,1,0:T(8,128)} %convolution_bitcast_fusion.2, f32[1,512,4096]{2,1,0:T(8,128)S(1)} %convolution_bitcast_fusion.3), kind=kLoop, calls=%fused_computation | loop fusion | flops 4194304 | bytes 33554432 | tf_op jit(solution)/shard_map/stack | solution.py:109
  421.3 7.5 %reduce-scatter.20.cloned.1.call-done = f32[32,512]{1,0:T(8,128)} async-done(((f32[128,512]{1,0:T(8,128)}), f32[32,512]{1,0:T(8,128)}) %reduce-scatter.20.cloned.1.call-update) | async-done | bytes 65552 | tf_op jit(solution)/shard_map/reduce_scatter | solution.py:91
  428.8 1.0 multiply_reduce_fusion.1
  429.9 12.0 %psum.45 = f32[32]{0:T(128)S(1)} all-reduce(f32[32]{0:T(128)S(1)} %get-tuple-element.5), channel_id=1, replica_groups=mesh['row'=4,'col'=8] {'col'}, use_global_device_ids=true, to_apply=%region_14.0 | all-reduce | flops 32 | bytes 256 | tf_op jit(solution)/shard_map/psum | solution.py:101
  441.9 0.9 add_convert_fusion
  442.8 0.6 all_to_all.44
  443.5 3.3 all-to-all-start.2
  446.8 9.0 %all-reduce = (f32[1,512]{1,0:T(1,128)S(1)}, f32[1,512]{1,0:T(1,128)S(1)}) all-reduce(f32[1,512]{1,0:T(1,128)S(1)} %bitcast.68, f32[1,512]{1,0:T(1,128)S(1)} %bitcast.69), channel_id=1, replica_groups=mesh['row'=4,'col'=8] {'row'}, use_global_device_ids=true, to_apply=%region_18.0 | all-reduce | flops 1024 | bytes 8192 | tf_op jit(solution)/shard_map/psum | solution.py:102
  456.5 0.6 copy.18
  (47 shorter events, 1.9 us)
Async XLA Ops:
  7.2 111.7 %copy-start.4 = (bf16[4,4096]{1,0:T(4,128)(2,1)S(1)}, bf16[4,4096]{1,0:T(4,128)(2,1)}, u32[]{:S(2)}) copy-start(bf16[4,4096]{1,0:T(4,128)(2,1)} %param.8) | copy-start | bytes 98308
  7.2 10.0 %all-to-all-start.1 = ((bf16[4,8,512]{2,0,1:T(4,128)(2,1)}), bf16[4,8,512]{2,0,1:T(4,128)(2,1)S(1)}, u32[]{:S(2)}, u32[]{:S(2)}) async-start(bf16[4,8,512]{2,0,1:T(4,128)(2,1)} %bitcast.66), calls=%async_computation.1 | async-start | bytes 65536 | tf_op jit(solution)/shard_map/all_to_all | solution.py:32
  12.4 76.4 %reduce-scatter.8.cloned.1.call-start = ((), (), s32[]{:S(2)}) async-start(), calls=%async_computation.10 | async-start | bytes 2359296 | tf_op jit(solution)/shard_map/reduce_scatter | solution.py:46
  47.3 67.6 %all-gather.5.cloned.1.call-start = ((), (), s32[]{:S(2)}) async-start(), calls=%async_computation.11 | async-start | bytes 1179648 | tf_op jit(solution)/shard_map/all_gather | solution.py:52
  90.5 54.8 %reduce-scatter.10.cloned.1.call-start = ((), (), s32[]{:S(2)}) async-start(), calls=%async_computation.12 | async-start | bytes 327680 | tf_op jit(solution)/shard_map/reduce_scatter | solution.py:57
  118.9 67.4 %reduce-scatter.12.cloned.1.call-start = ((), (), s32[]{:S(2)}) async-start(), calls=%async_computation.13 | async-start | bytes 2359296 | tf_op jit(solution)/shard_map/reduce_scatter | solution.py:76
  145.2 86.4 %reduce-scatter.14.cloned.1.call-start = ((), (), s32[]{:S(2)}) async-start(), calls=%async_computation.14 | async-start | bytes 2359296 | tf_op jit(solution)/shard_map/reduce_scatter | solution.py:46
  175.9 177.1 %copy-start.2 = (f32[16,4096]{1,0:T(8,128)S(1)}, f32[16,4096]{1,0:T(8,128)}, u32[]{:S(2)}) copy-start(f32[16,4096]{1,0:T(8,128)} %reduce-scatter.8.cloned.1.call-done) | copy-start | bytes 786436
  175.9 81.5 %all-gather.7.cloned.1.call-start = ((), (), s32[]{:S(2)}) async-start(), calls=%async_computation.15 | async-start | bytes 1179648 | tf_op jit(solution)/shard_map/all_gather | solution.py:85
  233.5 48.5 %reduce-scatter.16.cloned.1.call-start = ((), (), s32[]{:S(2)}) async-start(), calls=%async_computation.16 | async-start | bytes 327680 | tf_op jit(solution)/shard_map/reduce_scatter | solution.py:91
  257.4 97.6 %copy-start.1 = (bf16[128,4096]{1,0:T(8,128)(2,1)S(1)}, bf16[128,4096]{1,0:T(8,128)(2,1)}, u32[]{:S(2)}) copy-start(bf16[128,4096]{1,0:T(8,128)(2,1)} %all-gather.7.cloned.1.call-done) | copy-start | bytes 3145732
  262.3 90.7 %reduce-scatter.18.cloned.1.call-start = ((), (), s32[]{:S(2)}) async-start(), calls=%async_computation.17 | async-start | bytes 2359296 | tf_op jit(solution)/shard_map/reduce_scatter | solution.py:76
  314.6 64.4 %all-gather.11.cloned.1.call-start = ((), (), s32[]{:S(2)}) async-start(), calls=%async_computation.20 | async-start | bytes 1179648 | tf_op jit(solution)/shard_map/all_gather | solution.py:52
  315.4 88.9 %all-gather.9.cloned.1.call-start = ((), (), s32[]{:S(2)}) async-start(), calls=%async_computation.18 | async-start | bytes 1179648 | tf_op jit(solution)/shard_map/all_gather | solution.py:85
  354.8 26.7 %copy-start = (bf16[128,4096]{1,0:T(8,128)(2,1)S(1)}, bf16[128,4096]{1,0:T(8,128)(2,1)}, u32[]{:S(2)}) copy-start(bf16[128,4096]{1,0:T(8,128)(2,1)} %all-gather.5.cloned.1.call-done) | copy-start | bytes 3145732
  354.8 74.0 %reduce-scatter.20.cloned.1.call-start = ((), (), s32[]{:S(2)}) async-start(), calls=%async_computation.19 | async-start | bytes 327680 | tf_op jit(solution)/shard_map/reduce_scatter | solution.py:91
  411.6 30.3 %copy-start.3 = (f32[32,512]{1,0:T(8,128)S(1)}, f32[32,512]{1,0:T(8,128)}, u32[]{:S(2)}) copy-start(f32[32,512]{1,0:T(8,128)} %reduce-scatter.16.cloned.1.call-done) | copy-start | bytes 196612
  443.5 13.0 %all-to-all-start.2 = ((bf16[8,4,512]{2,1,0:T(4,128)(2,1)}), bf16[8,4,512]{2,1,0:T(4,128)(2,1)S(1)}, u32[]{:S(2)}, u32[]{:S(2)}) async-start(bf16[8,4,512]{2,1,0:T(4,128)(2,1)} %all_to_all.44), calls=%async_computation.9 | async-start | bytes 65536 | tf_op jit(solution)/shard_map/all_to_all | solution.py:104
Sparse Core Ops, SparseCore 0:
  47.4 41.2 reduce-scatter.7
  91.4 23.4 all-gather.4
  119.0 20.6 reduce-scatter.9
  145.3 40.8 reduce-scatter.11
  190.3 41.2 reduce-scatter.13
  233.9 23.4 all-gather.6
  262.4 19.6 reduce-scatter.15
  314.7 38.2 reduce-scatter.17
  355.5 23.4 all-gather.10
  380.7 23.4 all-gather.8
  409.2 19.6 reduce-scatter.19
where the time goes:
time: 465 us; the launch traced here: 464 us
  waiting for transfers between devices  249 us (54%)
  blocking collectives  119 us (26%)
  matrix products  42.8 us (9%)
  other arithmetic  27.4 us (6%)
  between operations  14.7 us (3%)
  starting transfers between devices  9.16 us (2%)
    reduce_scatter x2, waiting for transfers between devices, on_device(): lax.psum_scatter(jnp.dot(normed_all, up_block, preferred_element_type=jnp...  86.7 us
    reduce_scatter x2, waiting for transfers between devices, on_device(): lax.psum_scatter(lax.dot_general(grad_all, down_block, contract_cols, pre...  47.9 us
    all_gather x2, waiting for transfers between devices, on_device(): lax.all_gather(gelu_value(pre_rows).astype(jnp.bfloat16), 'col', axis=0,...  43.2 us
    all_gather x2, waiting for transfers between devices, on_device(): grad_pre_all = lax.all_gather(grad_pre, 'col', axis=0, tiled=True)  38.9 us
    all_gather x2, blocking collectives, on_device(): lax.all_gather(grad_stream.astype(jnp.bfloat16), 'row', axis=0, tiled=True)  27.4 us
    reduce_scatter x2, waiting for transfers between devices, on_device(): lax.psum_scatter(lax.dot_general(grad_pre_all, up_block, contract_cols, p...  27.3 us
    all_gather x2, blocking collectives, on_device(): normed_all = lax.all_gather(normed, 'row', axis=0, tiled=True)  27.1 us
    psum x2, blocking collectives, on_device(): inner_sum = lax.psum(jnp.sum(weighted * unit_rows, axis=1), 'col')  24 us
  transfers between devices with their start and end apart: 13, of which 11 were waited for; matrix products, arithmetic and copies ran while one was open for 9% of the time, Pallas kernels for 0%

commit v1 on v0

v1 whole, which is shorter than its diff:
```python
import functools

import jax
import jax.numpy as jnp
from jax import lax
from jax.experimental import pallas as pl
from jax.experimental.pallas import tpu as pltpu
from jax.sharding import PartitionSpec as P

epsilon_norm = 1e-06
gelu_scale = 0.7978845608028654
cubic_term = 0.044715
BF = jnp.bfloat16
F32 = jnp.float32
MESH = pl.DeviceIdType.MESH


def gelu_parts(v):
    t = jnp.tanh(gelu_scale * (v + cubic_term * v * v * v))
    value = 0.5 * v * (1.0 + t)
    slope = 0.5 * (1.0 + t) + 0.5 * v * (1.0 - t * t) * gelu_scale * (1.0 + 3.0 * cubic_term * v * v)
    return value, slope


def dot_nn(a, b):
    return jnp.dot(a, b, preferred_element_type=F32)


def dot_nt(a, b):
    return lax.dot_general(a, b, (((1,), (1,)), ((), ())), preferred_element_type=F32)


def dot_tn(a, b):
    return lax.dot_general(a, b, (((0,), (0,)), ((), ())), preferred_element_type=F32)


def to_row(column):
    wide = jnp.broadcast_to(column, (column.shape[0], 128))
    return jnp.transpose(wide)[0:8]


def to_column(row):
    return jnp.transpose(jnp.broadcast_to(row[0:1], (128, row.shape[1])))


class Counter:
    def __init__(self):
        self.n = 0

    def take(self, k):
        at = self.n
        self.n += k
        return at


def sem_total(R, C):
    nk = C // 2
    return 4 * 2 * nk + 4 * 2 * nk + 4 * (C - 1) + 2 * R + 3 * R + 2 * R + 3 * R + 64


def layers_kernel(R, C, both, gain, up_h, down_h, normed_o, gradb_o, hid_o, dpre_o, grad_o, gsum_o,
                  up, down, xa, gb, hid, dpre, core_s, core_r, chip_s, chip_r, acc, stats, inner,
                  row_s, row_r, rowx, normed_v, pre_v, slope_v, dh_v, stream_v, wsem, osem, ssem, rsem):
    L, T, Dc = both.shape
    H = up.shape[2]
    Hc = H // C
    Tr = T // R
    D = Dc * C
    nk = C // 2
    r, c = lax.axis_index("row"), lax.axis_index("col")
    k, core = c // 2, c % 2
    sib = k * 2 + (1 - core)
    ids = Counter()
    sends = []

    def chip_peer(m):
        out, b = k, 1
        while b < nk:
            out = out + b * ((m // b) % 2) * (1 - 2 * ((k // b) % 2))
            b *= 2
        return out

    def copy(src, dst, at, **where):
        return pltpu.make_async_remote_copy(src_ref=src, dst_ref=dst, send_sem=ssem.at[at], recv_sem=rsem.at[at],
                                            device_id=where, device_id_type=MESH)

    def send(src, dst, at, **where):
        one = copy(src, dst, at, **where)
        one.start()
        sends.append(one)

    def load(i, src, dst):
        one = pltpu.make_async_copy(src, dst, wsem.at[i])
        one.start()
        return one

    w_up0 = load(0, up_h.at[0], up.at[0])
    w_down1 = load(1, down_h.at[1], down.at[1])
    w_down0 = load(2, down_h.at[0], down.at[0])
    w_up1 = load(3, up_h.at[1], up.at[1])

    barrier = pltpu.get_barrier_semaphore()
    for d in range(1, C):
        pl.semaphore_signal(barrier, inc=1, device_id={"col": (c + d) % C}, device_id_type=MESH)
    for d in range(1, R):
        pl.semaphore_signal(barrier, inc=1, device_id={"row": (r + d) % R}, device_id_type=MESH)
    pl.semaphore_wait(barrier, C - 1 + R - 1)

    outs = []

    def emit(src, dst):
        one = pltpu.make_async_copy(src, dst, osem.at[len(outs)])
        one.start()
        outs.append(one)

    def stat_send(u, value):
        base = ids.take(C)
        stats[u, c] = value
        for d in range(1, C):
            send(stats.at[u, c], stats.at[u, c], base + d, col=(c + d) % C)
        return base

    def stat_sum(u, base):
        for d in range(1, C):
            frm = (c + C - d) % C
            copy(stats.at[u, frm], stats.at[u, frm], base + d, col=frm).wait_recv()
        return jnp.sum(stats[u], axis=0)

    def order():
        return list(range(nk - 1, 0, -1)) + [0]

    def rs_core(u, chunk, m, base):
        core_s[u, m] = chunk(chip_peer(m) * 2 + (1 - core)).astype(BF)
        send(core_s.at[u, m], core_r.at[u, m], base + m, col=sib)

    def rs_own(u, chunk, m, base):
        part = chunk(chip_peer(m) * 2 + core)
        copy(core_s.at[u, m], core_r.at[u, m], base + m, col=sib).wait_recv()
        return part + core_r[u, m].astype(F32)

    def rs_start(u, chunk):
        base = ids.take(2 * nk)
        ms = order()
        rs_core(u, chunk, ms[0], base)
        total = None
        for i, m in enumerate(ms):
            if i + 1 < nk:
                rs_core(u, chunk, ms[i + 1], base)
            total = rs_own(u, chunk, m, base)
            if m:
                chip_s[u, m] = total.astype(BF)
                send(chip_s.at[u, m], chip_r.at[u, m], base + nk + m, col=chip_peer(m) * 2 + core)
        return base, total

    def rs_end(u, base, total):
        for m in order()[:-1]:
            copy(chip_s.at[u, m], chip_r.at[u, m], base + nk + m, col=chip_peer(m) * 2 + core).wait_recv()
            total = total + chip_r[u, m].astype(F32)
        return total

    def ag_start(buf):
        base = ids.take(2 * nk)
        for m in order()[:-1]:
            send(buf.at[c], buf.at[c], base + m, col=chip_peer(m) * 2 + core)
        send(buf.at[c], buf.at[c], base, col=sib)
        return base

    def ag_each(buf, base, use):
        use(c)
        copy(buf.at[sib], buf.at[sib], base, col=sib).wait_recv()
        use(sib)
        for m in range(1, nk):
            peer = chip_peer(m) * 2
            mine, other = peer + core, peer + 1 - core
            copy(buf.at[mine], buf.at[mine], base + m, col=mine).wait_recv()
            send(buf.at[mine], buf.at[mine], base + nk + m, col=sib)
            use(mine)
            copy(buf.at[other], buf.at[other], base + nk + m, col=sib).wait_recv()
            use(other)

    def row_scatter(u, value_ref):
        base = ids.take(R)
        for d in range(1, R):
            peer = (r + d) % R
            row_s[u, d] = value_ref[pl.ds(pl.multiple_of(peer * Tr, Tr), Tr), :].astype(BF)
            send(row_s.at[u, d], row_r.at[u, d], base + d, row=peer)
        return base

    def row_sum(u, base, value_ref):
        total = value_ref[pl.ds(pl.multiple_of(r * Tr, Tr), Tr), :]
        for d in range(1, R):
            copy(row_s.at[u, d], row_r.at[u, d], base + d, row=(r + d) % R).wait_recv()
            total = total + row_r[u, d].astype(F32)
        return total

    def row_gather_start(buf):
        base = ids.take(R)
        for d in range(1, R):
            send(buf.at[r], buf.at[r], base + d, row=(r + d) % R)
        return base

    def row_gather_end(buf, base):
        for d in range(1, R):
            frm = (r + R - d) % R
            copy(buf.at[frm], buf.at[frm], base + d, row=frm).wait_recv()

    def lanes(j):
        return pl.ds(pl.multiple_of(j * Hc, Hc), Hc)

    gain0, gain1 = gain[0:1, :], gain[1:2, :]
    own = pl.ds(pl.multiple_of(r * Tr, Tr), Tr)

    tok = both[0].astype(F32)
    s0 = stat_send(0, to_row(jnp.sum(tok * tok, axis=1, keepdims=True)))
    xa[0] = (tok * gain0).astype(BF)
    w_up0.wait()
    base, total = rs_start(0, lambda j: dot_nn(xa[0], up[0, :, lanes(j)]))
    rstd0 = lax.rsqrt(to_column(stat_sum(0, s0)) / D + epsilon_norm)
    stream_v[0] = rstd0
    normed_v[0] = (both[0].astype(F32) * rstd0[:, 0:1] * gain0).astype(BF)
    emit(normed_v.at[0], normed_o.at[0])
    pre = rs_end(0, base, total) * rstd0[:, 0:1]
    value, slope = gelu_parts(pre)
    hid[0, c] = value.astype(BF)
    a0 = ag_start(hid.at[0])
    pre_v[0] = pre
    slope_v[0] = slope

    w_down1.wait()
    base_d, total_d = rs_start(1, lambda j: dot_nt(both[1], down[1, lanes(j), :]))
    dh_v[...] = total_d

    w_down0.wait()
    acc[...] = jnp.zeros_like(acc)

    def use_hidden(j):
        acc[...] += dot_nn(hid[0, j], down[0, lanes(j), :])

    ag_each(hid.at[0], a0, use_hidden)
    b = row_scatter(0, acc)
    stream1 = both[0, own, :].astype(F32) + row_sum(0, b, acc)
    rowx[0, r] = (stream1 * gain1).astype(BF)
    b = row_gather_start(rowx.at[0])
    emit(hid.at[0], hid_o.at[0])
    dh_v[...] = rs_end(1, base_d, dh_v[...])
    w_up1.wait()
    row_gather_end(rowx.at[0], b)

    xa[1] = rowx[0].reshape(T, Dc)
    raw = xa[1].astype(F32) / gain1
    s1 = stat_send(1, to_row(jnp.sum(raw * raw, axis=1, keepdims=True)))
    base, total = rs_start(2, lambda j: dot_nn(xa[1], up[1, :, lanes(j)]))
    rstd1 = lax.rsqrt(to_column(stat_sum(1, s1)) / D + epsilon_norm)
    stream_v[1] = rstd1
    normed_v[1] = (xa[1].astype(F32) * rstd1[:, 0:1]).astype(BF)
    emit(normed_v.at[1], normed_o.at[1])
    pre = rs_end(2, base, total) * rstd1[:, 0:1]
    value, slope = gelu_parts(pre)
    hid[1, c] = value.astype(BF)

    def backward(l, dhidden, pre, slope, stream_own, grad_above, gain_l, u):
        rounded = (dhidden * slope).astype(BF)
        dpre[l, c] = rounded
        a = ag_start(dpre.at[l])
        s = stat_send(2 + u, to_row(jnp.sum(rounded.astype(F32) * pre, axis=1, keepdims=True)))
        acc[...] = jnp.zeros_like(acc)

        def use(j):
            acc[...] += dot_nt(dpre[l, j], up[l, :, lanes(j)])

        ag_each(dpre.at[l], a, use)
        b = row_scatter(1 + u, acc)
        inner[u, r] = stat_sum(2 + u, s)
        bi = row_gather_start(inner.at[u])
        emit(dpre.at[l], dpre_o.at[l])
        a_late = ag_start(hid.at[1]) if l == 1 else None
        dnormed = row_sum(1 + u, b, acc)
        row_gather_end(inner.at[u], bi)
        stream_v[2 + u] = to_column(jnp.sum(inner[u], axis=0))
        inner_own = stream_v[2 + u, own, :][:, 0:1] / D
        rstd_own = stream_v[l, own, :][:, 0:1]
        unit = stream_own * rstd_own
        gsum_o[l:l + 1, :] = jnp.sum(dnormed * unit, axis=0, keepdims=True)
        return grad_above + rstd_own * (dnormed * gain_l - unit * inner_own), a_late

    top = both[1, own, :].astype(F32)
    grad1, a_late = backward(1, dh_v[...], pre, slope, stream1, top, gain1, 0)
    rowx[1, r] = grad1.astype(BF)
    b = row_gather_start(rowx.at[1])
    ag_each(hid.at[1], a_late, lambda j: None)
    emit(hid.at[1], hid_o.at[1])
    row_gather_end(rowx.at[1], b)
    gb[...] = rowx[1].reshape(T, Dc)
    emit(gb, gradb_o)
    base, total = rs_start(3, lambda j: dot_nt(gb[...], down[0, lanes(j), :]))
    dhidden = rs_end(3, base, total)
    grad0, _ = backward(0, dhidden, pre_v[0], slope_v[0], both[0, own, :].astype(F32), grad1, gain0, 1)
    grad_o[...] = grad0.astype(BF)
    for one in sends:
        one.wait_send()
    for one in outs:
        one.wait()


def run_layers(R, C, both, gain, up, down):
    _, T, Dc = both.shape
    L, _, H = up.shape
    Hc, Tr, nk = H // C, T // R, C // 2
    n = sem_total(R, C)
    any_spec = pl.BlockSpec(memory_space=pl.ANY)
    vm = pl.BlockSpec(memory_space=pltpu.VMEM)
    S = jax.ShapeDtypeStruct
    flops = 2 * T * Dc * H * 7
    return pl.pallas_call(
        functools.partial(layers_kernel, R, C),
        out_shape=(S((L, T, Dc), BF), S((T, Dc), BF), S((L, C, T, Hc), BF), S((L, C, T, Hc), BF),
                   S((Tr, Dc), BF), S((L, Dc), F32)),
        in_specs=[vm, vm, any_spec, any_spec],
        out_specs=(any_spec, any_spec, any_spec, any_spec, vm, vm),
        scratch_shapes=[
            pltpu.VMEM(up.shape, BF), pltpu.VMEM(down.shape, BF),
            pltpu.VMEM((L, T, Dc), BF), pltpu.VMEM((T, Dc), BF),
            pltpu.VMEM((L, C, T, Hc), BF), pltpu.VMEM((L, C, T, Hc), BF),
            pltpu.VMEM((4, nk, T, Hc), BF), pltpu.VMEM((4, nk, T, Hc), BF),
            pltpu.VMEM((4, nk, T, Hc), BF), pltpu.VMEM((4, nk, T, Hc), BF),
            pltpu.VMEM((T, Dc), F32),
            pltpu.VMEM((4, C, 8, T), F32), pltpu.VMEM((2, R, 8, T), F32),
            pltpu.VMEM((3, R, Tr, Dc), BF), pltpu.VMEM((3, R, Tr, Dc), BF),
            pltpu.VMEM((2, R, Tr, Dc), BF),
            pltpu.VMEM((L, T, Dc), BF),
            pltpu.VMEM((1, T, Hc), F32), pltpu.VMEM((1, T, Hc), F32), pltpu.VMEM((T, Hc), F32),
            pltpu.VMEM((4, T, 128), F32),
            pltpu.SemaphoreType.DMA((4,)), pltpu.SemaphoreType.DMA((8,)),
            pltpu.SemaphoreType.DMA((n,)), pltpu.SemaphoreType.DMA((n,)),
        ],
        compiler_params=pltpu.CompilerParams(collective_id=0, has_side_effects=True,
                                             vmem_limit_bytes=56 * 1024 * 1024),
        cost_estimate=pl.CostEstimate(flops=flops, bytes_accessed=2 * up.size * 4, transcendentals=0),
        name="layers",
    )(both, gain, up, down)


def grads_kernel(normed, gradb, hid, dpre, up_g, down_g):
    up_g[0] = dot_tn(normed[0], dpre[0, 0])
    down_g[0] = dot_tn(hid[0, 0], gradb[0])


def run_grads(normed, gradb, hid, dpre):
    L, T, Dc = normed.shape
    _, C, _, Hc = hid.shape
    whole = pl.BlockSpec((1, T, Dc), lambda l, j: (l, 0, 0))
    chunk = pl.BlockSpec((1, 1, T, Hc), lambda l, j: (l, j, 0, 0))
    S = jax.ShapeDtypeStruct
    return pl.pallas_call(
        grads_kernel,
        grid=(L, C),
        out_shape=(S((L, Dc, C * Hc), F32), S((L, C * Hc, Dc), F32)),
        in_specs=[whole, whole, chunk, chunk],
        out_specs=(pl.BlockSpec((1, Dc, Hc), lambda l, j: (l, 0, j)),
                   pl.BlockSpec((1, Hc, Dc), lambda l, j: (l, j, 0))),
        compiler_params=pltpu.CompilerParams(vmem_limit_bytes=32 * 1024 * 1024),
        cost_estimate=pl.CostEstimate(flops=4 * L * T * Dc * C * Hc, bytes_accessed=8 * L * Dc * C * Hc,
                                      transcendentals=0),
        name="grads",
    )(normed, gradb, hid, dpre)


def on_device(R, C, tokens, counts, cotangent, up_weight, down_weight, norm_gain):
    slots = tokens.shape[0]
    live = (jnp.arange(slots, dtype=jnp.int32) < counts[0]).astype(BF)[:, None]
    both = jnp.stack([tokens, cotangent * live])
    both = lax.all_to_all(both, "col", split_axis=2, concat_axis=1, tiled=True)
    both = lax.all_gather(both, "row", axis=1, tiled=True)
    normed, gradb0, hid, dpre, grad0, gsum = run_layers(R, C, both, norm_gain, up_weight, down_weight)
    token_grad = lax.all_to_all(grad0, "col", split_axis=0, concat_axis=1, tiled=True)
    gain_grad = lax.psum(gsum, "row")
    up_g, down_g = run_grads(normed, jnp.stack([gradb0, both[1]]), hid, dpre)
    return token_grad, up_g, down_g, gain_grad


def solution(mesh):
    R, C = mesh.shape["row"], mesh.shape["col"]
    return jax.shard_map(
        functools.partial(on_device, R, C),
        mesh=mesh,
        in_specs=(P(("row", "col"), None), P(("row", "col")), P(("row", "col"), None),
                  P(None, "col", "row"), P(None, "row", "col"), P(None, "col")),
        out_specs=(P(("row", "col"), None), P(None, "col", "row"), P(None, "row", "col"), P(None, "col")),
        check_vma=False,
    )
```

time: 465 us -> 174 us (0.37)
  waiting for transfers between devices: 249 us -> 0.01 us
  Pallas kernels: 0 us -> 112 us
  blocking collectives: 119 us -> 34.6 us
  matrix products: 42.8 us -> 0 us
  other arithmetic: 27.4 us -> 2.59 us
  local copies, waits for them, and re-layouts: 2.16 us -> 19.7 us
  between operations: 14.7 us -> 1.37 us
  starting transfers between devices: 9.16 us -> 3.34 us
    reduce_scatter x7 -> x0, waiting for transfers between devices: 162 us -> none  [the longest x2 86.7 us: on_device(): lax.psum_scatter(jnp.dot(normed_all, up_block, preferred_element_type=jnp...]
    pallas_call x0 -> x2, Pallas kernels: none -> 112 us  [the longest x1 98.1 us: run_layers(): pl.pallas_call(functools.partial(layers_kernel, R, C), out_shape=(S((L, T...]
    all_gather x4 -> x0, waiting for transfers between devices: 82.1 us -> none  [the longest x2 43.2 us: on_device(): lax.all_gather(gelu_value(pre_rows).astype(jnp.bfloat16), 'col', axis=0,...]
    psum x5 -> x1, blocking collectives: 56.8 us -> 10.4 us  [on_device(): gain_grad = lax.psum(gsum, 'row')]
    dot_general x11 -> x0, matrix products: 42.8 us -> none  [the longest x2 9.97 us: on_device(): lax.dot_general(grad_all, down_block, contract_cols, preferred_element_ty...]
    all_gather x4 -> x1, blocking collectives: 54.5 us -> 14.3 us  [on_device(): both = lax.all_gather(both, 'row', axis=1, tiled=True)]
    another operation x3, other arithmetic: 16.7 us -> 2.58 us  [the longest x2 1.65 us: on_device(): both = jnp.stack([tokens, cotangent * live])]
    unnamed x11 -> x13, local copies, waits for them, and re-layouts: 0.64 us -> 13.9 us
  transfers between devices with their start and end apart: 13 -> 1, of which waited for: 11 -> 0; matrix products, arithmetic and copies ran while one was open for 9% -> 1% of each run, Pallas kernels for 0% -> 8%
where the time goes in v1:
time: 174 us; the launch traced here: 173 us
  Pallas kernels  112 us (64%)
  blocking collectives  34.6 us (20%)
  local copies, waits for them, and re-layouts  19.7 us (11%)
  starting transfers between devices  3.34 us (2%)
  other arithmetic  2.59 us (1%)
    pallas_call x1, Pallas kernels, run_layers(): pl.pallas_call(functools.partial(layers_kernel, R, C), out_shape=(S((L, T...  98.1 us
    all_gather x1, blocking collectives, on_device(): both = lax.all_gather(both, 'row', axis=1, tiled=True)  14.3 us
    unnamed x13, local copies, waits for them, and re-layouts  13.9 us
    pallas_call x1, Pallas kernels, run_grads(): pl.pallas_call(grads_kernel, grid=(L, C), out_shape=(S((L, Dc, C * Hc), F...  13.6 us
    psum x1, blocking collectives, on_device(): gain_grad = lax.psum(gsum, 'row')  10.4 us
    all_to_all x1, blocking collectives, on_device(): both = lax.all_to_all(both, 'col', split_axis=2, concat_axis=1, tiled=True)  9.99 us
  transfers between devices with their start and end apart: 1, of which 0 were waited for; matrix products, arithmetic and copies ran while one was open for 1% of the time, Pallas kernels for 8%

profile of v1, /device:TPU:0, one launch (start us, length us, event | category | flops | bytes accessed | tf_op | source)
XLA Modules:
  0.0 173.3 jit_solution(6475852550282819054)
XLA Ops:
  1.3 0.8 multiply_bitcast_fusion
  2.1 0.8 pad_maximum_fusion.1
  2.9 2.9 %copy.16 = bf16[2,4,4096]{1,0,2:T(2,128)(2,1)S(1)} copy(bf16[2,4,4096]{2,1,0:T(4,128)(2,1)S(1)} %pad_maximum_fusion.1) | data formatting | bytes 131072 | tf_op jit(solution)/shard_map/stack | solution.py:371
  5.9 4.0 %reshape.16 = bf16[8,2,2048]{2,1,0:T(2,128)(2,1)S(1)} reshape(bf16[4096,2,4]{2,1,0:T(2,128)(2,1)S(1)} %bitcast.13) | data formatting | bytes 131072
  9.8 10.0 %all_to_all.37 = bf16[8,2,2048]{2,1,0:T(2,128)(2,1)S(1)} all-to-all(bf16[8,2,2048]{2,1,0:T(2,128)(2,1)S(1)} %reshape.16), channel_id=1, replica_groups=mesh['row'=4,'col'=8] {'col'}, dimensions={0} | all-to-all | bytes 131072 | tf_op jit(solution)/shard_map/all_to_all | solution.py:372
  19.8 4.5 %reshape.17 = bf16[4096,2,4]{2,1,0:T(2,128)(2,1)S(1)} reshape(bf16[8,2,2048]{2,1,0:T(2,128)(2,1)S(1)} %all_to_all.37) | data formatting | bytes 131072
  24.3 1.4 copy.17
  25.8 14.3 %all_gather.3.both = bf16[2,128,512]{2,1,0:T(8,128)(2,1)S(1)} all-gather(bf16[2,32,512]{2,1,0:T(8,128)(2,1)S(1)} %all_to_all.30), channel_id=1, replica_groups=mesh['row'=4,'col'=8] {'row'}, dimensions={1}, use_global_device_ids=true | all-gather | bytes 327680 | tf_op jit(solution)/shard_map/all_gather | solution.py:373
  40.1 0.0 copy-start.3
  40.1 0.7 copy-done.3
  40.8 98.1 %layers.1 = (bf16[2,128,512]{2,1,0:T(8,128)(2,1)}, bf16[128,512]{1,0:T(8,128)(2,1)}, bf16[2,8,128,512]{3,2,1,0:T(8,128)(2,1)}, bf16[2,8,128,512]{3,2,1,0:T(8,128...) custom-call(bf16[2,128,512]{2,1,0:T(8,128)(2,1)} %copy-done.3, f32[2,512]{1,0:T(2,128)} %gain.1, ...), custom_call_target="tpu_custom_call" | custom-call | flops 3758096384 | bytes 33554432 | tf_op jit(solution)/shard_map/layers/pallas_call | solution.py:314
  138.9 0.0 copy-start.4
  138.9 1.4 all_to_all.31
  140.3 3.3 %all-to-all-start.1 = ((bf16[8,4,512]{2,1,0:T(4,128)(2,1)}), bf16[8,4,512]{2,1,0:T(4,128)(2,1)S(1)}, u32[]{:S(2)}, u32[]{:S(2)}) async-start(bf16[8,4,512]{2,1,0:T(4,128)(2,1)} %all_to_all.31), calls=%async_computation.1 | async-start | bytes 65536 | tf_op jit(solution)/shard_map/all_to_all | solution.py:375
  143.7 0.9 pad_maximum_fusion.gradb
  144.6 0.0 copy-start
  144.6 1.6 copy-done
  146.2 0.0 copy-start.1
  146.2 1.6 copy-done.1
  147.8 0.0 copy-start.2
  147.8 0.9 copy-done.2
  148.7 13.6 %grads.1 = (f32[2,512,4096]{2,1,0:T(8,128)}, f32[2,4096,512]{2,1,0:T(8,128)}) custom-call(bf16[2,128,512]{2,1,0:T(8,128)(2,1)S(1)} %copy-done.2, bf16[2,128,512]{2,1,0:T(8,128)(2,1)S(1)} %pad_maximum_fusion.gradb, bf16[2,8,128,512]{3,2,1,0:T(8,128)(2,1)S(1)} %copy-done, bf16[2,8,128,512]{3,2,1,0:T(8,128)(2,1)S(1)} %copy-done.1), custom_call_target="tpu_custom_call" | custom-call | flops 2147483648 | bytes 33554432 | tf_op jit(solution)/shard_map/grads/pallas_call | solution.py:354
  162.3 0.0 copy-done.4
  162.3 10.4 %psum.7 = f32[2,512]{1,0:T(2,128)} all-reduce(f32[2,512]{1,0:T(2,128)S(1)} %copy-done.4), channel_id=1, replica_groups=mesh['row'=4,'col'=8] {'row'}, use_global_device_ids=true, to_apply=%region_0.0 | all-reduce | flops 1024 | bytes 8192 | tf_op jit(solution)/shard_map/psum | solution.py:376
  172.7 0.0 all-to-all-done.1
  172.7 0.6 copy.21
  (3 shorter events, 0.0 us)
Async XLA Ops:
  40.1 0.7 copy-start.3
  138.9 23.4 %copy-start.4 = (f32[2,512]{1,0:T(2,128)S(1)}, f32[2,512]{1,0:T(2,128)}, u32[]{:S(2)}) copy-start(f32[2,512]{1,0:T(2,128)} %get-tuple-element.19) | copy-start | bytes 12292
  140.3 32.4 %all-to-all-start.1 = ((bf16[8,4,512]{2,1,0:T(4,128)(2,1)}), bf16[8,4,512]{2,1,0:T(4,128)(2,1)S(1)}, u32[]{:S(2)}, u32[]{:S(2)}) async-start(bf16[8,4,512]{2,1,0:T(4,128)(2,1)} %all_to_all.31), calls=%async_computation.1 | async-start | bytes 65536 | tf_op jit(solution)/shard_map/all_to_all | solution.py:375
  144.6 1.6 copy-start
  146.2 1.6 copy-start.1
  147.8 0.9 copy-start.2

commit v2 on v1

--- a/solution.py
+++ b/solution.py
@@ -55,17 +55,18 @@
 
 def sem_total(R, C):
     nk = C // 2
-    return 4 * 2 * nk + 4 * 2 * nk + 4 * (C - 1) + 2 * R + 3 * R + 2 * R + 3 * R + 64
-
-
-def layers_kernel(R, C, both, gain, up_h, down_h, normed_o, gradb_o, hid_o, dpre_o, grad_o, gsum_o,
-                  up, down, xa, gb, hid, dpre, core_s, core_r, chip_s, chip_r, acc, stats, inner,
+    return 16 * nk + 6 * C + 12 * R
+
+
+def layers_kernel(R, C, entry, gain, up_h, down_h, normed_o, gradb_o, hid_o, dpre_o, grad_o, gsum_o,
+                  up, down, ent, tokx, topx, fin_s, fin_r, gains, xa, gb, hid, dpre, core_s, core_r, chip_s, chip_r, acc, stats, inner,
                   row_s, row_r, rowx, normed_v, pre_v, slope_v, dh_v, stream_v, wsem, osem, ssem, rsem):
-    L, T, Dc = both.shape
-    H = up.shape[2]
+    L, Dc, H = up.shape
     Hc = H // C
+    T = xa.shape[1]
     Tr = T // R
     D = Dc * C
+    half = entry.shape[0] // 2
     nk = C // 2
     r, c = lax.axis_index("row"), lax.axis_index("col")
     k, core = c // 2, c % 2
@@ -106,6 +107,16 @@
         pl.semaphore_signal(barrier, inc=1, device_id={"row": (r + d) % R}, device_id_type=MESH)
     pl.semaphore_wait(barrier, C - 1 + R - 1)
 
+    base_e = ids.take(C)
+
+    def features(j):
+        return pl.ds(pl.multiple_of(j * Dc, Dc), Dc)
+
+    for d in range(1, C):
+        peer = (c + d) % C
+        send(entry.at[:, features(peer)], ent.at[c], base_e + d, col=peer)
+    ent[c] = entry[:, features(c)]
+
     outs = []
 
     def emit(src, dst):
@@ -138,7 +149,7 @@
         copy(core_s.at[u, m], core_r.at[u, m], base + m, col=sib).wait_recv()
         return part + core_r[u, m].astype(F32)
 
-    def rs_start(u, chunk):
+    def rs_start(u, chunk, later=False):
         base = ids.take(2 * nk)
         ms = order()
         rs_core(u, chunk, ms[0], base)
@@ -149,8 +160,13 @@
             total = rs_own(u, chunk, m, base)
             if m:
                 chip_s[u, m] = total.astype(BF)
+            if m and not later:
                 send(chip_s.at[u, m], chip_r.at[u, m], base + nk + m, col=chip_peer(m) * 2 + core)
         return base, total
+
+    def rs_send(u, base):
+        for m in order()[:-1]:
+            send(chip_s.at[u, m], chip_r.at[u, m], base + nk + m, col=chip_peer(m) * 2 + core)
 
     def rs_end(u, base, total):
         for m in order()[:-1]:
@@ -210,14 +226,37 @@
     gain0, gain1 = gain[0:1, :], gain[1:2, :]
     own = pl.ds(pl.multiple_of(r * Tr, Tr), Tr)
 
-    tok = both[0].astype(F32)
+    for d in range(1, C):
+        frm = (c + C - d) % C
+        copy(entry.at[:, features(frm)], ent.at[frm], base_e + d, col=frm).wait_recv()
+    first = lax.broadcasted_iota(jnp.int32, (2 * half, Dc), 0) < half
+    tok_rows, top_rows = [], []
+    for i in range(C // 2):
+        low, high = ent[2 * i], ent[2 * i + 1]
+        tok_rows.append(jnp.where(first, low, pltpu.roll(high, half, 0)))
+        top_rows.append(jnp.where(first, pltpu.roll(low, half, 0), high))
+    tok_own = jnp.concatenate(tok_rows, axis=0)
+    top = jnp.concatenate(top_rows, axis=0)
+    tokx[r] = tok_own.astype(BF)
+    b_tok = row_gather_start(tokx)
+    topx[r] = top.astype(BF)
+    b_top = row_gather_start(topx)
+    row_gather_end(tokx, b_tok)
+
+    tok = tokx[...].reshape(T, Dc).astype(F32)
     s0 = stat_send(0, to_row(jnp.sum(tok * tok, axis=1, keepdims=True)))
     xa[0] = (tok * gain0).astype(BF)
     w_up0.wait()
     base, total = rs_start(0, lambda j: dot_nn(xa[0], up[0, :, lanes(j)]))
+    row_gather_end(topx, b_top)
+    gb[1] = topx[...].reshape(T, Dc)
+    emit(gb.at[1], gradb_o.at[1])
+    w_down1.wait()
+    base_d, total_d = rs_start(1, lambda j: dot_nt(gb[1], down[1, lanes(j), :]), later=True)
+    dh_v[...] = total_d
     rstd0 = lax.rsqrt(to_column(stat_sum(0, s0)) / D + epsilon_norm)
     stream_v[0] = rstd0
-    normed_v[0] = (both[0].astype(F32) * rstd0[:, 0:1] * gain0).astype(BF)
+    normed_v[0] = (tok * rstd0[:, 0:1] * gain0).astype(BF)
     emit(normed_v.at[0], normed_o.at[0])
     pre = rs_end(0, base, total) * rstd0[:, 0:1]
     value, slope = gelu_parts(pre)
@@ -226,10 +265,6 @@
     pre_v[0] = pre
     slope_v[0] = slope
 
-    w_down1.wait()
-    base_d, total_d = rs_start(1, lambda j: dot_nt(both[1], down[1, lanes(j), :]))
-    dh_v[...] = total_d
-
     w_down0.wait()
     acc[...] = jnp.zeros_like(acc)
 
@@ -238,7 +273,8 @@
 
     ag_each(hid.at[0], a0, use_hidden)
     b = row_scatter(0, acc)
-    stream1 = both[0, own, :].astype(F32) + row_sum(0, b, acc)
+    rs_send(1, base_d)
+    stream1 = tokx[r].astype(F32) + row_sum(0, b, acc)
     rowx[0, r] = (stream1 * gain1).astype(BF)
     b = row_gather_start(rowx.at[0])
     emit(hid.at[0], hid_o.at[0])
@@ -280,31 +316,49 @@
         inner_own = stream_v[2 + u, own, :][:, 0:1] / D
         rstd_own = stream_v[l, own, :][:, 0:1]
         unit = stream_own * rstd_own
-        gsum_o[l:l + 1, :] = jnp.sum(dnormed * unit, axis=0, keepdims=True)
-        return grad_above + rstd_own * (dnormed * gain_l - unit * inner_own), a_late
-
-    top = both[1, own, :].astype(F32)
-    grad1, a_late = backward(1, dh_v[...], pre, slope, stream1, top, gain1, 0)
+        gains[l, r] = jnp.broadcast_to(jnp.sum(dnormed * unit, axis=0, keepdims=True), (8, Dc))
+        bg = row_gather_start(gains.at[l])
+        return grad_above + rstd_own * (dnormed * gain_l - unit * inner_own), a_late, bg
+
+    grad1, a_late, bg1 = backward(1, dh_v[...], pre, slope, stream1, top, gain1, 0)
     rowx[1, r] = grad1.astype(BF)
     b = row_gather_start(rowx.at[1])
     ag_each(hid.at[1], a_late, lambda j: None)
     emit(hid.at[1], hid_o.at[1])
     row_gather_end(rowx.at[1], b)
-    gb[...] = rowx[1].reshape(T, Dc)
-    emit(gb, gradb_o)
-    base, total = rs_start(3, lambda j: dot_nt(gb[...], down[0, lanes(j), :]))
+    gb[0] = rowx[1].reshape(T, Dc)
+    emit(gb.at[0], gradb_o.at[0])
+    base, total = rs_start(3, lambda j: dot_nt(gb[0], down[0, lanes(j), :]))
     dhidden = rs_end(3, base, total)
-    grad0, _ = backward(0, dhidden, pre_v[0], slope_v[0], both[0, own, :].astype(F32), grad1, gain0, 1)
-    grad_o[...] = grad0.astype(BF)
+    grad0, _, bg0 = backward(0, dhidden, pre_v[0], slope_v[0], tokx[r].astype(F32), grad1, gain0, 1)
+
+    fin_s[...] = grad0.reshape(C // 2, 2 * half, Dc)
+    base_x = ids.take(C)
+    for d in range(1, C):
+        peer = (c + d) % C
+        send(fin_s.at[peer // 2], fin_r.at[c], base_x + d, col=peer)
+    fin_r[c] = fin_s[k]
+    for l, bg in ((1, bg1), (0, bg0)):
+        row_gather_end(gains.at[l], bg)
+        gsum_o[l:l + 1, :] = jnp.sum(gains[l], axis=0)[0:1]
+    for d in range(1, C):
+        frm = (c + C - d) % C
+        copy(fin_s.at[k], fin_r.at[frm], base_x + d, col=frm).wait_recv()
+    upper = core == 1
+    for j in range(C):
+        block = fin_r[j]
+        block = jnp.where(upper, pltpu.roll(block, half, 0), block)
+        grad_o[:, j * Dc:(j + 1) * Dc] = block[0:half].astype(BF)
     for one in sends:
         one.wait_send()
     for one in outs:
         one.wait()
 
 
-def run_layers(R, C, both, gain, up, down):
-    _, T, Dc = both.shape
-    L, _, H = up.shape
+def run_layers(R, C, entry, gain, up, down):
+    L, Dc, H = up.shape
+    half = entry.shape[0] // 2
+    T = half * R * C
     Hc, Tr, nk = H // C, T // R, C // 2
     n = sem_total(R, C)
     any_spec = pl.BlockSpec(memory_space=pl.ANY)
@@ -313,13 +367,16 @@
     flops = 2 * T * Dc * H * 7
     return pl.pallas_call(
         functools.partial(layers_kernel, R, C),
-        out_shape=(S((L, T, Dc), BF), S((T, Dc), BF), S((L, C, T, Hc), BF), S((L, C, T, Hc), BF),
-                   S((Tr, Dc), BF), S((L, Dc), F32)),
+        out_shape=(S((L, T, Dc), BF), S((L, T, Dc), BF), S((L, C, T, Hc), BF), S((L, C, T, Hc), BF),
+                   S((half, C * Dc), BF), S((L, Dc), F32)),
         in_specs=[vm, vm, any_spec, any_spec],
         out_specs=(any_spec, any_spec, any_spec, any_spec, vm, vm),
         scratch_shapes=[
             pltpu.VMEM(up.shape, BF), pltpu.VMEM(down.shape, BF),
-            pltpu.VMEM((L, T, Dc), BF), pltpu.VMEM((T, Dc), BF),
+            pltpu.VMEM((C, 2 * half, Dc), F32), pltpu.VMEM((R, Tr, Dc), BF), pltpu.VMEM((R, Tr, Dc), BF),
+            pltpu.VMEM((C // 2, 2 * half, Dc), F32), pltpu.VMEM((C, 2 * half, Dc), F32),
+            pltpu.VMEM((L, R, 8, Dc), F32),
+            pltpu.VMEM((L, T, Dc), BF), pltpu.VMEM((L, T, Dc), BF),
             pltpu.VMEM((L, C, T, Hc), BF), pltpu.VMEM((L, C, T, Hc), BF),
             pltpu.VMEM((4, nk, T, Hc), BF), pltpu.VMEM((4, nk, T, Hc), BF),
             pltpu.VMEM((4, nk, T, Hc), BF), pltpu.VMEM((4, nk, T, Hc), BF),
@@ -337,7 +394,7 @@
                                              vmem_limit_bytes=56 * 1024 * 1024),
         cost_estimate=pl.CostEstimate(flops=flops, bytes_accessed=2 * up.size * 4, transcendentals=0),
         name="layers",
-    )(both, gain, up, down)
+    )(entry, gain, up, down)
 
 
 def grads_kernel(normed, gradb, hid, dpre, up_g, down_g):
@@ -358,7 +415,7 @@
         in_specs=[whole, whole, chunk, chunk],
         out_specs=(pl.BlockSpec((1, Dc, Hc), lambda l, j: (l, 0, j)),
                    pl.BlockSpec((1, Hc, Dc), lambda l, j: (l, j, 0))),
-        compiler_params=pltpu.CompilerParams(vmem_limit_bytes=32 * 1024 * 1024),
+        compiler_params=pltpu.CompilerParams(vmem_limit_bytes=60 * 1024 * 1024),
         cost_estimate=pl.CostEstimate(flops=4 * L * T * Dc * C * Hc, bytes_accessed=8 * L * Dc * C * Hc,
                                       transcendentals=0),
         name="grads",
@@ -368,13 +425,9 @@
 def on_device(R, C, tokens, counts, cotangent, up_weight, down_weight, norm_gain):
     slots = tokens.shape[0]
     live = (jnp.arange(slots, dtype=jnp.int32) < counts[0]).astype(BF)[:, None]
-    both = jnp.stack([tokens, cotangent * live])
-    both = lax.all_to_all(both, "col", split_axis=2, concat_axis=1, tiled=True)
-    both = lax.all_gather(both, "row", axis=1, tiled=True)
-    normed, gradb0, hid, dpre, grad0, gsum = run_layers(R, C, both, norm_gain, up_weight, down_weight)
-    token_grad = lax.all_to_all(grad0, "col", split_axis=0, concat_axis=1, tiled=True)
-    gain_grad = lax.psum(gsum, "row")
-    up_g, down_g = run_grads(normed, jnp.stack([gradb0, both[1]]), hid, dpre)
+    entry = jnp.concatenate([tokens, cotangent * live]).astype(F32)
+    normed, gradb, hid, dpre, token_grad, gain_grad = run_layers(R, C, entry, norm_gain, up_weight, down_weight)
+    up_g, down_g = run_grads(normed, gradb, hid, dpre)
     return token_grad, up_g, down_g, gain_grad
 
 

time: 174 us -> 136 us (0.78)
  blocking collectives: 34.6 us -> 0 us
  local copies, waits for them, and re-layouts: 19.7 us -> 2.65 us
  Pallas kernels: 112 us -> 129 us
  starting transfers between devices: 3.34 us -> 0 us
    all_gather x1 -> x0, blocking collectives: 14.3 us -> none  [on_device(): both = lax.all_gather(both, 'row', axis=1, tiled=True)]
    pallas_call x1, Pallas kernels: 98.1 us -> 112 us  [run_layers(): pl.pallas_call(functools.partial(layers_kernel, R, C), out_shape=(S((L, T...]
    unnamed x13 -> x2, local copies, waits for them, and re-layouts: 13.9 us -> 2.65 us
    psum x1 -> x0, blocking collectives: 10.4 us -> none  [on_device(): gain_grad = lax.psum(gsum, 'row')]
    all_to_all x1 -> x0, blocking collectives: 9.99 us -> none  [on_device(): both = lax.all_to_all(both, 'col', split_axis=2, concat_axis=1, tiled=True)]
    pallas_call x1, Pallas kernels: 13.6 us -> 16.9 us  [run_grads(): pl.pallas_call(grads_kernel, grid=(L, C), out_shape=(S((L, Dc, C * Hc), F...]
    all_to_all x1 -> x0, starting transfers between devices: 3.34 us -> none  [on_device(): lax.all_to_all(grad0, 'col', split_axis=0, concat_axis=1, tiled=True)]
    another operation x1 -> x0, local copies, waits for them, and re-layouts: 2.91 us -> none  [on_device(): both = jnp.stack([tokens, cotangent * live])]
  transfers between devices with their start and end apart: 1 -> 0, of which waited for: 0 -> 0; matrix products, arithmetic and copies ran while one was open for 1% -> 0% of each run, Pallas kernels for 8% -> 0%
where the time goes in v2:
time: 136 us
  Pallas kernels  129 us (95%)
  local copies, waits for them, and re-layouts  2.65 us (2%)
  other arithmetic  2.3 us (2%)
    pallas_call x1, Pallas kernels, run_layers(): pl.pallas_call(functools.partial(layers_kernel, R, C), out_shape=(S((L, T...  112 us
    pallas_call x1, Pallas kernels, run_grads(): pl.pallas_call(grads_kernel, grid=(L, C), out_shape=(S((L, Dc, C * Hc), F...  16.9 us

profile of v2, /device:TPU:0, one launch (start us, length us, event | category | flops | bytes accessed | tf_op | source)
XLA Modules:
  0.0 135.5 jit_solution(1055038521520065237)
XLA Ops:
  1.3 0.8 broadcast_multiply_fusion
  2.1 1.4 %maximum_convert_fusion.entry = f32[8,4096]{1,0:T(8,128)} fusion(bf16[4,4096]{1,0:T(4,128)(2,1)S(1)} %broadcast_multiply_fusion, bf16[4,4096]{1,0:T(4,128)(2,1)} %param.6), kind=kLoop, calls=%fused_computation | loop fusion | flops 131072 | bytes 196608 | tf_op jit(solution)/shard_map/convert_element_type | solution.py:428
  3.6 112.4 %layers.1 = (bf16[2,128,512]{2,1,0:T(8,128)(2,1)}, bf16[2,128,512]{2,1,0:T(8,128)(2,1)}, bf16[2,8,128,512]{3,2,1,0:T(8,128)(2,1)}, bf16[2,8,128,512]{3,2,1,0:T(8...) custom-call(f32[8,4096]{1,0:T(8,128)} %maximum_convert_fusion.entry, f32[2,512]{1,0:T(2,128)} %gain.1, ...), custom_call_target="tpu_custom_call" | custom-call | flops 3758096384 | bytes 33554432 | tf_op jit(solution)/shard_map/layers/pallas_call | solution.py:368
  116.0 16.9 %grads.1 = (f32[2,512,4096]{2,1,0:T(8,128)}, f32[2,4096,512]{2,1,0:T(8,128)}) custom-call(bf16[2,128,512]{2,1,0:T(8,128)(2,1)} %get-tuple-element.13.normed, bf16[2,128,512]{2,1,0:T(8,128)(2,1)} %get-tuple-element.14.gradb, bf16[2,8,128,512]{3,2,1,0:T(8,128)(2,1)} %get-tuple-element.15.hid, bf16[2,8,128,512]{3,2,1,0:T(8,128)(2,1)} %get-tuple-element.16.dpre), custom_call_target="tpu_custom_call" | custom-call | flops 2147483648 | bytes 33554432 | tf_op jit(solution)/shard_map/grads/pallas_call | solution.py:411
  132.9 1.4 %copy.13 = bf16[4,4096]{1,0:T(4,128)(2,1)} copy(bf16[4,4096]{1,0:T(4,128)(2,1)} %get-tuple-element.24) | data formatting | bytes 65536
  134.3 1.3 copy.14
  (1 shorter events, 0.0 us)

commit v3 on v2

--- a/solution.py
+++ b/solution.py
@@ -58,15 +58,15 @@
     return 16 * nk + 6 * C + 12 * R
 
 
-def layers_kernel(R, C, entry, gain, up_h, down_h, normed_o, gradb_o, hid_o, dpre_o, grad_o, gsum_o,
-                  up, down, ent, tokx, topx, fin_s, fin_r, gains, xa, gb, hid, dpre, core_s, core_r, chip_s, chip_r, acc, stats, inner,
+def layers_kernel(R, C, tokens, cotangent, counts, gain, up_h, down_h, normed_o, gradb_o, hid_o, dpre_o, grad_o, gsum_o,
+                  up, down, normed_t, hid_t, entry, ent, tokx, topx, fin_s, fin_r, gains, xa, gb, hid, dpre, core_s, core_r, chip_s, chip_r, acc, stats, inner,
                   row_s, row_r, rowx, normed_v, pre_v, slope_v, dh_v, stream_v, wsem, osem, ssem, rsem):
     L, Dc, H = up.shape
     Hc = H // C
     T = xa.shape[1]
     Tr = T // R
     D = Dc * C
-    half = entry.shape[0] // 2
+    half = tokens.shape[0]
     nk = C // 2
     r, c = lax.axis_index("row"), lax.axis_index("col")
     k, core = c // 2, c % 2
@@ -99,6 +99,11 @@
     w_down1 = load(1, down_h.at[1], down.at[1])
     w_down0 = load(2, down_h.at[0], down.at[0])
     w_up1 = load(3, up_h.at[1], up.at[1])
+
+    slot = lax.broadcasted_iota(jnp.int32, cotangent.shape, 0)
+    live = jnp.where(slot < counts[0], 1.0, 0.0)
+    entry[0:half, :] = tokens[...].astype(F32)
+    entry[half:2 * half, :] = cotangent[...].astype(F32) * live
 
     barrier = pltpu.get_barrier_semaphore()
     for d in range(1, C):
@@ -257,7 +262,8 @@
     rstd0 = lax.rsqrt(to_column(stat_sum(0, s0)) / D + epsilon_norm)
     stream_v[0] = rstd0
     normed_v[0] = (tok * rstd0[:, 0:1] * gain0).astype(BF)
-    emit(normed_v.at[0], normed_o.at[0])
+    normed_t[0] = jnp.transpose(normed_v[0])
+    emit(normed_t.at[0], normed_o.at[0])
     pre = rs_end(0, base, total) * rstd0[:, 0:1]
     value, slope = gelu_parts(pre)
     hid[0, c] = value.astype(BF)
@@ -277,7 +283,9 @@
     stream1 = tokx[r].astype(F32) + row_sum(0, b, acc)
     rowx[0, r] = (stream1 * gain1).astype(BF)
     b = row_gather_start(rowx.at[0])
-    emit(hid.at[0], hid_o.at[0])
+    for j in range(C):
+        hid_t[0, j] = jnp.transpose(hid[0, j])
+    emit(hid_t.at[0], hid_o.at[0])
     dh_v[...] = rs_end(1, base_d, dh_v[...])
     w_up1.wait()
     row_gather_end(rowx.at[0], b)
@@ -289,7 +297,8 @@
     rstd1 = lax.rsqrt(to_column(stat_sum(1, s1)) / D + epsilon_norm)
     stream_v[1] = rstd1
     normed_v[1] = (xa[1].astype(F32) * rstd1[:, 0:1]).astype(BF)
-    emit(normed_v.at[1], normed_o.at[1])
+    normed_t[1] = jnp.transpose(normed_v[1])
+    emit(normed_t.at[1], normed_o.at[1])
     pre = rs_end(2, base, total) * rstd1[:, 0:1]
     value, slope = gelu_parts(pre)
     hid[1, c] = value.astype(BF)
@@ -323,12 +332,16 @@
     grad1, a_late, bg1 = backward(1, dh_v[...], pre, slope, stream1, top, gain1, 0)
     rowx[1, r] = grad1.astype(BF)
     b = row_gather_start(rowx.at[1])
-    ag_each(hid.at[1], a_late, lambda j: None)
-    emit(hid.at[1], hid_o.at[1])
+
+    def turn(j):
+        hid_t[1, j] = jnp.transpose(hid[1, j])
+
     row_gather_end(rowx.at[1], b)
     gb[0] = rowx[1].reshape(T, Dc)
     emit(gb.at[0], gradb_o.at[0])
     base, total = rs_start(3, lambda j: dot_nt(gb[0], down[0, lanes(j), :]))
+    ag_each(hid.at[1], a_late, turn)
+    emit(hid_t.at[1], hid_o.at[1])
     dhidden = rs_end(3, base, total)
     grad0, _, bg0 = backward(0, dhidden, pre_v[0], slope_v[0], tokx[r].astype(F32), grad1, gain0, 1)
 
@@ -355,9 +368,9 @@
         one.wait()
 
 
-def run_layers(R, C, entry, gain, up, down):
+def run_layers(R, C, tokens, cotangent, counts, gain, up, down):
     L, Dc, H = up.shape
-    half = entry.shape[0] // 2
+    half = tokens.shape[0]
     T = half * R * C
     Hc, Tr, nk = H // C, T // R, C // 2
     n = sem_total(R, C)
@@ -367,12 +380,14 @@
     flops = 2 * T * Dc * H * 7
     return pl.pallas_call(
         functools.partial(layers_kernel, R, C),
-        out_shape=(S((L, T, Dc), BF), S((L, T, Dc), BF), S((L, C, T, Hc), BF), S((L, C, T, Hc), BF),
+        out_shape=(S((L, Dc, T), BF), S((L, T, Dc), BF), S((L, C, Hc, T), BF), S((L, C, T, Hc), BF),
                    S((half, C * Dc), BF), S((L, Dc), F32)),
-        in_specs=[vm, vm, any_spec, any_spec],
+        in_specs=[vm, vm, pl.BlockSpec(memory_space=pltpu.SMEM), vm, any_spec, any_spec],
         out_specs=(any_spec, any_spec, any_spec, any_spec, vm, vm),
         scratch_shapes=[
             pltpu.VMEM(up.shape, BF), pltpu.VMEM(down.shape, BF),
+            pltpu.VMEM((L, Dc, T), BF), pltpu.VMEM((L, C, Hc, T), BF),
+            pltpu.VMEM((2 * half, C * Dc), F32),
             pltpu.VMEM((C, 2 * half, Dc), F32), pltpu.VMEM((R, Tr, Dc), BF), pltpu.VMEM((R, Tr, Dc), BF),
             pltpu.VMEM((C // 2, 2 * half, Dc), F32), pltpu.VMEM((C, 2 * half, Dc), F32),
             pltpu.VMEM((L, R, 8, Dc), F32),
@@ -394,40 +409,48 @@
                                              vmem_limit_bytes=56 * 1024 * 1024),
         cost_estimate=pl.CostEstimate(flops=flops, bytes_accessed=2 * up.size * 4, transcendentals=0),
         name="layers",
-    )(entry, gain, up, down)
-
-
-def grads_kernel(normed, gradb, hid, dpre, up_g, down_g):
-    up_g[0] = dot_tn(normed[0], dpre[0, 0])
-    down_g[0] = dot_tn(hid[0, 0], gradb[0])
-
-
-def run_grads(normed, gradb, hid, dpre):
-    L, T, Dc = normed.shape
-    _, C, _, Hc = hid.shape
-    whole = pl.BlockSpec((1, T, Dc), lambda l, j: (l, 0, 0))
-    chunk = pl.BlockSpec((1, 1, T, Hc), lambda l, j: (l, j, 0, 0))
+    )(tokens, cotangent, counts, gain, up, down)
+
+
+def grads_kernel(normed, gradb, hid, dpre, token_in, gain_in, up_g, down_g, token_g, gain_g):
+    up_g[0] = dot_nn(normed[0], dpre[0, 0])
+    down_g[0] = dot_nn(hid[0, 0], gradb[0])
+
+    @pl.when((pl.program_id(0) == 0) & (pl.program_id(1) == 0))
+    def _():
+        token_g[...] = token_in[...]
+        gain_g[...] = gain_in[...]
+
+
+def run_grads(normed, gradb, hid, dpre, token, gain):
+    L, T, Dc = gradb.shape
+    _, C, _, Hc = dpre.shape
     S = jax.ShapeDtypeStruct
+    token_spec = pl.BlockSpec(token.shape, lambda l, j: (0, 0))
+    gain_spec = pl.BlockSpec(gain.shape, lambda l, j: (0, 0))
     return pl.pallas_call(
         grads_kernel,
         grid=(L, C),
-        out_shape=(S((L, Dc, C * Hc), F32), S((L, C * Hc, Dc), F32)),
-        in_specs=[whole, whole, chunk, chunk],
+        out_shape=(S((L, Dc, C * Hc), F32), S((L, C * Hc, Dc), F32), S(token.shape, BF), S(gain.shape, F32)),
+        in_specs=[pl.BlockSpec((1, Dc, T), lambda l, j: (l, 0, 0)),
+                  pl.BlockSpec((1, T, Dc), lambda l, j: (l, 0, 0)),
+                  pl.BlockSpec((1, 1, Hc, T), lambda l, j: (l, j, 0, 0)),
+                  pl.BlockSpec((1, 1, T, Hc), lambda l, j: (l, j, 0, 0)),
+                  token_spec, gain_spec],
         out_specs=(pl.BlockSpec((1, Dc, Hc), lambda l, j: (l, 0, j)),
-                   pl.BlockSpec((1, Hc, Dc), lambda l, j: (l, j, 0))),
+                   pl.BlockSpec((1, Hc, Dc), lambda l, j: (l, j, 0)),
+                   token_spec, gain_spec),
         compiler_params=pltpu.CompilerParams(vmem_limit_bytes=60 * 1024 * 1024),
         cost_estimate=pl.CostEstimate(flops=4 * L * T * Dc * C * Hc, bytes_accessed=8 * L * Dc * C * Hc,
                                       transcendentals=0),
         name="grads",
-    )(normed, gradb, hid, dpre)
+    )(normed, gradb, hid, dpre, token, gain)
 
 
 def on_device(R, C, tokens, counts, cotangent, up_weight, down_weight, norm_gain):
-    slots = tokens.shape[0]
-    live = (jnp.arange(slots, dtype=jnp.int32) < counts[0]).astype(BF)[:, None]
-    entry = jnp.concatenate([tokens, cotangent * live]).astype(F32)
-    normed, gradb, hid, dpre, token_grad, gain_grad = run_layers(R, C, entry, norm_gain, up_weight, down_weight)
-    up_g, down_g = run_grads(normed, gradb, hid, dpre)
+    normed, gradb, hid, dpre, token, gain = run_layers(R, C, tokens, cotangent, counts, norm_gain,
+                                                       up_weight, down_weight)
+    up_g, down_g, token_grad, gain_grad = run_grads(normed, gradb, hid, dpre, token, gain)
     return token_grad, up_g, down_g, gain_grad
 
 

time: 136 us -> 132 us (0.971)
  local copies, waits for them, and re-layouts: 2.65 us -> 0 us
  other arithmetic: 2.3 us -> 0 us
    unnamed x2 -> x0, local copies, waits for them, and re-layouts: 2.65 us -> none
    convert_element_type x2 -> x0, other arithmetic: 1.45 us -> none  [the longest x1 1.45 us: on_device(): entry = jnp.concatenate([tokens, cotangent * live]).astype(F32)]
where the time goes in v3:
time: 132 us; the launch traced here: 131 us
  Pallas kernels  130 us (98%)
    pallas_call x1, Pallas kernels, run_layers(): pl.pallas_call(functools.partial(layers_kernel, R, C), out_shape=(S((L, D...  112 us
    pallas_call x1, Pallas kernels, run_grads(): pl.pallas_call(grads_kernel, grid=(L, C), out_shape=(S((L, Dc, C * Hc), F...  17.6 us

profile of v3, /device:TPU:0, one launch (start us, length us, event | category | flops | bytes accessed | tf_op | source)
XLA Modules:
  0.0 131.3 jit_solution(1613812624949556884)
XLA Ops:
  1.3 112.4 %layers.1 = (bf16[2,512,128]{2,1,0:T(8,128)(2,1)}, bf16[2,128,512]{2,1,0:T(8,128)(2,1)}, bf16[2,8,512,128]{3,2,1,0:T(8,128)(2,1)}, bf16[2,8,128,512]{3,2,1,0:T(8...) custom-call(bf16[4,4096]{1,0:T(4,128)(2,1)} %tokens.1, bf16[4,4096]{1,0:T(4,128)(2,1)} %cotangent.1, ...), custom_call_target="tpu_custom_call" | custom-call | flops 3758096384 | bytes 33554432 | tf_op jit(solution)/shard_map/layers/pallas_call | solution.py:381
  113.7 17.6 %grads.1 = (f32[2,512,4096]{2,1,0:T(8,128)}, f32[2,4096,512]{2,1,0:T(8,128)}, bf16[4,4096]{1,0:T(4,128)(2,1)}, f32[2,512]{1,0:T(2,128)}) custom-call(bf16[2,512,128]{2,1,0:T(8,128)(2,1)} %get-tuple-element.14.normed, bf16[2,128,512]{2,1,0:T(8,128)(2,1)} %get-tuple-element.15.gradb, bf16[2,8,512,128]{3,2,1,0:T(8,128)(2,1)} %get-tuple-element.16.hid, ...), custom_call_target="tpu_custom_call" | custom-call | flops 2147483648 | bytes 33554432 | tf_op jit(solution)/shard_map/grads/pallas_call | solution.py:431
